TPU v7x, 32 devices: a whole 2x2x4 slice. The times are simulated.
32 devices in a mesh: group: 4 (over y, x), key: 8 (over z, core).
Axes of the slice: x: 2, y: 2, z: 4, core: 2. Of those that a mesh axis runs over, the one named last changes fastest.
Arguments:
- src_desc: bfloat16 [8192, 256], P(('group', 'key'))
- tgt_desc: bfloat16 [16384, 256], P('key')
- src_weight: float32 [8192], P(('group', 'key')), may hold values from 0.05 to 20
- tgt_weight: float32 [16384], P('key'), may hold values from 0.05 to 20
- tgt_dual: float32 [16384], P('key'), may hold values from -1.2 to 1.2
- pair_blocks: int32 [4, 8, 2, 64], P('group', 'key'), may hold values from 0 to 7, as said below
- pair_count: int32 [4, 8], P('group', 'key'), may hold values from 8 to 64, as said below
Outputs:
- src_dual: float32 [8192], P(('group', 'key'))
- tgt_dual_new: float32 [16384], P('key')
Inputs may be any that keep to these rules, and one draw needn't show every extreme that they name: `pair_blocks`: row 0 holds source clusters 0 to 7, row 1 target clusters 0 to 7; the live slots of one device are distinct pairs; every source cluster and every target cluster is in some live pair. `pair_count`: live slots come first.
All inputs are finite; a program needn't handle non-finite values.
Results may differ from a plain program's by a relative error of at most 0.0003.
Values may be sent and summed in bfloat16 or wider, within the bound.
A program may use at most 64 MiB of HBM per device.

v0:
```python
import functools
import math

import jax
import jax.numpy as jnp
from jax import lax
from jax.experimental import pallas as pl
from jax.experimental.pallas import tpu as pltpu
from jax.sharding import PartitionSpec as P

CLUSTER = 256
HALF = 128
ENTROPY = 0.05
NEG_FLOOR = -1e30
LOG2E = 1.0 / math.log(2.0)
TO_BASE2 = LOG2E / ENTROPY
FROM_BASE2 = ENTROPY / LOG2E
MESH = pl.DeviceIdType.MESH
NT = (((1,), (1,)), ((), ()))


def nt_dot(a, b):
    return lax.dot_general(a, b, NT, preferred_element_type=jnp.float32)


def square_row(rows):
    wide = rows.astype(jnp.float32)
    square = wide * wide
    high = square.astype(jnp.bfloat16)
    low = (square - high.astype(jnp.float32)).astype(jnp.bfloat16)
    ones = jnp.ones((8, rows.shape[1]), jnp.bfloat16)
    return (nt_dot(ones, high) + nt_dot(ones, low))[0:1] * (1.0 / rows.shape[1])


def spread(row):
    return jnp.broadcast_to(row, (HALF, HALF)).T


def block_sums(left, right, scale, offset_ref, start):
    inner = nt_dot(left, right) * scale
    offset = offset_ref[pl.ds(start, CLUSTER), :]
    tops, totals = [], []
    for half in range(CLUSTER // HALF):
        score = inner[:, half * HALF : (half + 1) * HALF] + offset
        top = jnp.max(score, axis=0, keepdims=True)
        totals.append(jnp.sum(jnp.exp2(score - top), axis=0, keepdims=True))
        tops.append(top)
    return jnp.concatenate(tops, axis=1), jnp.concatenate(totals, axis=1)


def merge(tops, totals, listed):
    tops = jnp.where(listed, tops, NEG_FLOOR)
    best = jnp.max(tops, axis=0, keepdims=True)
    total = jnp.sum(jnp.where(listed, totals * jnp.exp2(tops - best), 0.0), axis=0, keepdims=True)
    return best + jnp.log(total) * LOG2E


def kernel(groups, keys, src_ref, tgt_ref, sw_ref, tw_ref, td_ref, pb_ref, pc_ref, so_ref, to_ref,
           gs, plse, wg, tl, acol, bcol, brow, sqt, mt, lt,
           s_send, s_recv, p_send, p_recv, w_send, w_recv, t_send, t_recv):
    g, k = lax.axis_index("group"), lax.axis_index("key")
    pos, core = k // 2, k % 2
    n_pos = keys // 2
    width = src_ref.shape[1]
    n_tgt = tgt_ref.shape[0] // CLUSTER
    scale = 2.0 / width * TO_BASE2

    def key_peer(r):
        return lax.rem(k + r, keys)

    barrier = pltpu.get_barrier_semaphore()

    def greet(r, carry):
        pl.semaphore_signal(barrier, inc=1, device_id=(g, key_peer(r)), device_id_type=MESH)
        return carry

    lax.fori_loop(1, keys, greet, 0)
    for r in range(1, groups):
        pl.semaphore_signal(barrier, inc=1, device_id=(lax.rem(g + r, groups), k), device_id_type=MESH)
    gs[k] = src_ref[...]
    wg[k] = jnp.log(jnp.concatenate([sw_ref[0:1, :], sw_ref[1:2, :]], axis=1)) * LOG2E
    pl.semaphore_wait(barrier, keys + groups - 2)

    def shard(slot, lane):
        target = (2 * (pos - 1) + core, 2 * (pos + 1) + core, 2 * pos + 1 - core)[lane]
        return pltpu.make_async_remote_copy(
            src_ref=gs.at[slot], dst_ref=gs.at[slot], send_sem=s_send.at[lane, slot],
            recv_sem=s_recv.at[slot], device_id=(g, target), device_id_type=MESH)

    def weights(r):
        return pltpu.make_async_remote_copy(
            src_ref=wg.at[k], dst_ref=wg.at[k], send_sem=w_send.at[r], recv_sem=w_recv.at[k],
            device_id=(g, key_peer(r)), device_id_type=MESH)

    def weights_from(r):
        peer = key_peer(r)
        return pltpu.make_async_remote_copy(
            src_ref=wg.at[peer], dst_ref=wg.at[peer], send_sem=w_send.at[r], recv_sem=w_recv.at[peer],
            device_id=(g, peer), device_id_type=MESH)

    @pl.when(pos > 0)
    def _():
        shard(k, 0).start()

    @pl.when(pos < n_pos - 1)
    def _():
        shard(k, 1).start()

    shard(k, 2).start()

    def send_weights(r, carry):
        weights(r).start()
        return carry

    lax.fori_loop(1, keys, send_weights, 0)

    def prepare(t, carry):
        sq = square_row(tgt_ref[pl.ds(pl.multiple_of(t * CLUSTER, CLUSTER), CLUSTER), :])
        sqt[pl.ds(t, 1), :] = sq
        for half in range(2):
            row = (td_ref[pl.ds(2 * t + half, 1), :] - sq[:, half * HALF : (half + 1) * HALF]) * TO_BASE2
            acol[pl.ds(pl.multiple_of(t * CLUSTER + half * HALF, HALF), HALF), :] = spread(row)
        return carry

    lax.fori_loop(0, n_tgt, prepare, 0)

    slots = pb_ref.shape[1]
    live = lax.broadcasted_iota(jnp.int32, (1, slots), 1) < pc_ref[...]
    src_ids = jnp.where(live, pb_ref[0:1, :], -1)
    tgt_ids = pb_ref[1:2, :]

    def listed_rows(rows, row_ids, other_ids, other):
        hit = (lax.broadcasted_iota(jnp.int32, (rows, slots), 0) == row_ids) & (other_ids == other)
        return jnp.sum(jnp.where(hit, 1.0, 0.0), axis=1, keepdims=True) > 0.0

    def first(slot):
        src = gs[slot]
        for t in range(n_tgt):
            top, total = block_sums(tgt_ref[t * CLUSTER : (t + 1) * CLUSTER, :], src, scale, acol, t * CLUSTER)
            mt[t : t + 1, :] = top
            lt[t : t + 1, :] = total
        listed = listed_rows(n_tgt, tgt_ids, src_ids, slot)
        plse[k, pl.ds(slot, 1), :] = merge(mt[0:n_tgt, :], lt[0:n_tgt, :], listed)

    def distance(d, carry):
        before, after = pos - d, pos + d

        @pl.when((d > 0) & (before >= 0))
        def _():
            slot = 2 * before + core
            shard(slot, 1).wait_recv()

            @pl.when(pos < n_pos - 1)
            def _():
                shard(slot, 1).start()

            shard(slot, 2).start()

        @pl.when((d > 0) & (after < n_pos))
        def _():
            slot = 2 * after + core
            shard(slot, 0).wait_recv()

            @pl.when(pos > 0)
            def _():
                shard(slot, 0).start()

            shard(slot, 2).start()

        def job(w, carry):
            forward, other = w % 2, w // 2
            at = pos + d * (2 * forward - 1)

            @pl.when((at >= 0) & (at < n_pos) & ((d > 0) | (forward == 0)))
            def _():
                slot = 2 * at + core + other * (1 - 2 * core)

                @pl.when(other == 1)
                def _():
                    shard(slot, 2).wait_recv()

                first(slot)

            return carry

        return lax.fori_loop(0, 4, job, carry)

    lax.fori_loop(0, n_pos, distance, 0)

    def partial(r):
        return pltpu.make_async_remote_copy(
            src_ref=plse.at[k], dst_ref=plse.at[k], send_sem=p_send.at[r], recv_sem=p_recv.at[k],
            device_id=(g, key_peer(r)), device_id_type=MESH)

    def partial_from(r):
        peer = key_peer(r)
        return pltpu.make_async_remote_copy(
            src_ref=plse.at[peer], dst_ref=plse.at[peer], send_sem=p_send.at[r], recv_sem=p_recv.at[peer],
            device_id=(g, peer), device_id_type=MESH)

    def send_partial(r, carry):
        partial(r).start()
        return carry

    def take_partial(r, carry):
        weights_from(r).wait_recv()
        partial_from(r).wait_recv()
        return carry

    lax.fori_loop(1, keys, send_partial, 0)
    own_sq = square_row(src_ref[...])
    lax.fori_loop(1, keys, take_partial, 0)

    every = plse[...]
    best = jnp.max(every, axis=0)
    total = jnp.sum(jnp.exp2(every - best[None]), axis=0)
    brow[...] = wg[...].reshape(keys, CLUSTER) - (best + jnp.log(total) * LOG2E)
    own = brow[pl.ds(k, 1), :] * FROM_BASE2 + own_sq
    so_ref[0:1, :] = own[:, :HALF]
    so_ref[1:2, :] = own[:, HALF:]

    def columns(s, carry):
        row = brow[pl.ds(s, 1), :]
        for half in range(2):
            bcol[pl.ds(pl.multiple_of(s * CLUSTER + half * HALF, HALF), HALF), :] = spread(
                row[:, half * HALF : (half + 1) * HALF])
        return carry

    lax.fori_loop(0, keys, columns, 0)

    step = math.gcd(keys, 8)

    def second(t, carry):
        tgt = tgt_ref[pl.ds(pl.multiple_of(t * CLUSTER, CLUSTER), CLUSTER), :]

        def some(c, carry):
            for j in range(step):
                s = c * step + j
                top, total = block_sums(gs[s], tgt, scale, bcol, pl.multiple_of(s * CLUSTER, CLUSTER))
                mt[pl.ds(s, 1), :] = top
                lt[pl.ds(s, 1), :] = total
            return carry

        lax.fori_loop(0, keys // step, some, 0)
        listed = listed_rows(keys, src_ids, tgt_ids, t)
        tl[g, pl.ds(t, 1), :] = merge(mt[0:keys, :], lt[0:keys, :], listed)
        return carry

    lax.fori_loop(0, n_tgt, second, 0)

    def column(r):
        return pltpu.make_async_remote_copy(
            src_ref=tl.at[g], dst_ref=tl.at[g], send_sem=t_send.at[r], recv_sem=t_recv.at[g],
            device_id=(lax.rem(g + r, groups), k), device_id_type=MESH)

    def column_from(r):
        peer = lax.rem(g + r, groups)
        return pltpu.make_async_remote_copy(
            src_ref=tl.at[peer], dst_ref=tl.at[peer], send_sem=t_send.at[r], recv_sem=t_recv.at[peer],
            device_id=(peer, k), device_id_type=MESH)

    for r in range(1, groups):
        column(r).start()

    def sent_shards(p, carry):
        slot = 2 * p + core

        @pl.when((pos > 0) & (p >= pos))
        def _():
            shard(slot, 0).wait_send()

        @pl.when((pos < n_pos - 1) & (p <= pos))
        def _():
            shard(slot, 1).wait_send()

        shard(slot, 2).wait_send()
        return carry

    def sent_rows(r, carry):
        weights(r).wait_send()
        partial(r).wait_send()
        return carry

    lax.fori_loop(0, n_pos, sent_shards, 0)
    lax.fori_loop(1, keys, sent_rows, 0)
    for r in range(1, groups):
        column_from(r).wait_recv()

    every = tl[...]
    best = jnp.max(every, axis=0)
    total = jnp.sum(jnp.exp2(every - best[None]), axis=0)
    lse = best + jnp.log(total) * LOG2E
    new = sqt[...] - lse * FROM_BASE2
    for t in range(n_tgt):
        for half in range(2):
            at = 2 * t + half
            to_ref[at : at + 1, :] = (
                new[t : t + 1, half * HALF : (half + 1) * HALF] + jnp.log(tw_ref[at : at + 1, :]) * ENTROPY)
    for r in range(1, groups):
        column(r).wait_send()


def local(groups, keys, src_desc, tgt_desc, src_weight, tgt_weight, tgt_dual, pair_blocks, pair_count):
    rows, width = tgt_desc.shape
    n_tgt = rows // CLUSTER
    slots = pair_blocks.shape[3]
    f32 = jnp.float32
    dma = pltpu.SemaphoreType.DMA
    most = max(keys, n_tgt)
    blocks = 2 * keys * n_tgt
    src_dual, tgt_new = pl.pallas_call(
        functools.partial(kernel, groups, keys),
        out_shape=(jax.ShapeDtypeStruct((CLUSTER // HALF, HALF), f32),
                   jax.ShapeDtypeStruct((rows // HALF, HALF), f32)),
        in_specs=[pl.BlockSpec(memory_space=pltpu.VMEM)] * 7,
        out_specs=[pl.BlockSpec(memory_space=pltpu.VMEM)] * 2,
        scratch_shapes=[
            pltpu.VMEM((keys, CLUSTER, width), jnp.bfloat16),
            pltpu.VMEM((keys, keys, CLUSTER), f32),
            pltpu.VMEM((keys, 1, CLUSTER), f32),
            pltpu.VMEM((groups, n_tgt, CLUSTER), f32),
            pltpu.VMEM((rows, HALF), f32),
            pltpu.VMEM((keys * CLUSTER, HALF), f32),
            pltpu.VMEM((keys, CLUSTER), f32),
            pltpu.VMEM((n_tgt, CLUSTER), f32),
            pltpu.VMEM((most, CLUSTER), f32),
            pltpu.VMEM((most, CLUSTER), f32),
            dma((3, keys)), dma((keys,)),
            dma((keys,)), dma((keys,)),
            dma((keys,)), dma((keys,)),
            dma((groups,)), dma((groups,)),
        ],
        compiler_params=pltpu.CompilerParams(
            collective_id=0, has_side_effects=True, vmem_limit_bytes=44 * 1024 * 1024),
        cost_estimate=pl.CostEstimate(
            flops=blocks * 2 * CLUSTER * CLUSTER * width, bytes_accessed=2 * rows * width,
            transcendentals=blocks * CLUSTER * CLUSTER),
    )(
        src_desc, tgt_desc,
        src_weight.reshape(CLUSTER // HALF, HALF),
        tgt_weight.reshape(rows // HALF, HALF),
        tgt_dual.reshape(rows // HALF, HALF),
        pair_blocks.reshape(2, slots), pair_count.reshape(1, 1),
    )
    return src_dual.reshape(CLUSTER), tgt_new.reshape(rows)


def solution(mesh):
    groups, keys = mesh.shape["group"], mesh.shape["key"]
    in_specs = (
        P(("group", "key"), None),
        P("key", None),
        P(("group", "key")),
        P("key"),
        P("key"),
        P("group", "key", None, None),
        P("group", "key"),
    )
    out_specs = (P(("group", "key")), P("key"))
    return jax.shard_map(functools.partial(local, groups, keys), mesh=mesh, in_specs=in_specs,
                         out_specs=out_specs, check_vma=False)
```

profile of v0, /device:TPU:0, one launch (start us, length us, event | category | flops | bytes accessed | tf_op | source)
XLA Modules:
  0.0 41.9 jit_solution(9281507655440246084)
XLA Ops:
  0.6 0.0 copy-start.2
  1.3 0.0 copy-start.4
  1.3 0.0 copy-done.2
  1.3 0.7 %copy-done.4 = f32[256]{0:T(256)S(1)} copy-done((f32[256]{0:T(256)S(1)}, f32[256]{0:T(256)}, u32[]{:S(2)}) %copy-start.4) | copy-done | bytes 1048
  2.0 0.0 copy-start
  2.0 1.2 %copy-done = bf16[2048,256]{1,0:T(8,128)(2,1)S(1)} copy-done((bf16[2048,256]{1,0:T(8,128)(2,1)S(1)}, bf16[2048,256]{1,0:T(8,128)(2,1)}, u32[]{:S(2)}) %copy-start) | copy-done | bytes 1048600
  3.2 0.0 copy-start.1
  3.2 0.9 %copy-done.1 = bf16[256,256]{1,0:T(8,128)(2,1)S(1)} copy-done((bf16[256,256]{1,0:T(8,128)(2,1)S(1)}, bf16[256,256]{1,0:T(8,128)(2,1)}, u32[]{:S(2)}) %copy-start.1) | copy-done | bytes 131096
  4.1 0.0 copy-start.3
  4.1 0.7 %copy-done.3 = f32[2048]{0:T(1024)S(1)} copy-done((f32[2048]{0:T(1024)S(1)}, f32[2048]{0:T(1024)}, u32[]{:S(2)}) %copy-start.3) | copy-done | bytes 8216
  4.8 0.0 copy-start.5
  4.8 0.7 %copy-done.5 = s32[1,1,2,64]{3,2,1,0:T(2,128)S(1)} copy-done((s32[1,1,2,64]{3,2,1,0:T(2,128)S(1)}, s32[1,1,2,64]{3,2,1,0:T(2,128)}, u32[]{:S(2)}) %copy-start.5) | copy-done | bytes 536
  5.5 35.3 %shard_map.86 = (f32[2,128]{1,0:T(2,128)S(1)}, f32[16,128]{1,0:T(8,128)S(1)}) custom-call(bf16[256,256]{1,0:T(8,128)(2,1)S(1)} %copy-done.1, bf16[2048,256]{1,0:T(8,128)(2,1)S(1)} %copy-done, f32[2,128]{1,0:T(2,128)S(1)} %bitcast.10, f32[16,128]{1,0:T(8,128)S(1)} %bitcast.8, f32[16,128]{1,0:T(8,128)S(1)} %bitcast.9, s32[2,64]{1,0:T(2,128)S(1)} %bitcast.11, ...), custom_call_target="tpu_custom_call" | custom-call | flops 4294967296 | bytes 1048576 | tf_op jit(solution)/shard_map/pallas_call | solution.py:311
  40.8 0.6 %copy.12 = f32[256]{0:T(256)} copy(f32[256]{0:T(256)S(1)} %bitcast.7) | data formatting | bytes 2048
  41.3 0.6 %copy.13 = f32[2048]{0:T(1024)} copy(f32[2048]{0:T(1024)S(1)} %bitcast.6) | data formatting | bytes 16384
Async XLA Ops:
  0.6 0.7 %copy-start.2 = (f32[2048]{0:T(1024)S(1)}, f32[2048]{0:T(1024)}, u32[]{:S(2)}) copy-start(f32[2048]{0:T(1024)} %param.10) | copy-start | bytes 24580
  1.3 0.7 %copy-start.4 = (f32[256]{0:T(256)S(1)}, f32[256]{0:T(256)}, u32[]{:S(2)}) copy-start(f32[256]{0:T(256)} %param.9) | copy-start | bytes 3076
  2.0 1.2 %copy-start = (bf16[2048,256]{1,0:T(8,128)(2,1)S(1)}, bf16[2048,256]{1,0:T(8,128)(2,1)}, u32[]{:S(2)}) copy-start(bf16[2048,256]{1,0:T(8,128)(2,1)} %tgt_ref.1) | copy-start | bytes 3145732
  3.2 0.9 %copy-start.1 = (bf16[256,256]{1,0:T(8,128)(2,1)S(1)}, bf16[256,256]{1,0:T(8,128)(2,1)}, u32[]{:S(2)}) copy-start(bf16[256,256]{1,0:T(8,128)(2,1)} %src_ref.1) | copy-start | bytes 393220
  4.1 0.7 %copy-start.3 = (f32[2048]{0:T(1024)S(1)}, f32[2048]{0:T(1024)}, u32[]{:S(2)}) copy-start(f32[2048]{0:T(1024)} %param.11) | copy-start | bytes 24580
  4.8 0.7 %copy-start.5 = (s32[1,1,2,64]{3,2,1,0:T(2,128)S(1)}, s32[1,1,2,64]{3,2,1,0:T(2,128)}, u32[]{:S(2)}) copy-start(s32[1,1,2,64]{3,2,1,0:T(2,128)} %param.12) | copy-start | bytes 1540
where the time goes:
time: 42.3 us; the launch traced here: 41.9 us
  Pallas kernels  35.3 us (83%)
  local copies, waits for them, and re-layouts  5.34 us (13%)
  between operations  1.32 us (3%)
    pallas_call x1, Pallas kernels, local(): pl.pallas_call(functools.partial(kernel, groups, keys), out_shape=(jax.Sh...  35.3 us
    unnamed x14, local copies, waits for them, and re-layouts  5.34 us

commit v1 on v0

--- a/solution.py
+++ b/solution.py
@@ -55,18 +55,24 @@
     return best + jnp.log(total) * LOG2E
 
 
-def kernel(groups, keys, src_ref, tgt_ref, sw_ref, tw_ref, td_ref, pb_ref, pc_ref, so_ref, to_ref,
-           gs, plse, wg, tl, acol, bcol, brow, sqt, mt, lt,
+def kernel(groups, keys, src_hbm, tgt_hbm, sw_hbm, tw_hbm, td_hbm, pb_hbm, pc_ref, so_ref, to_ref,
+           tgt_ref, sw_ref, tw_ref, td_ref, pb_ref, load_sem, gs, plse, wg, tl, acol, bcol, brow, sqt, mt, lt,
            s_send, s_recv, p_send, p_recv, w_send, w_recv, t_send, t_recv):
     g, k = lax.axis_index("group"), lax.axis_index("key")
     pos, core = k // 2, k % 2
     n_pos = keys // 2
-    width = src_ref.shape[1]
+    width = tgt_ref.shape[1]
     n_tgt = tgt_ref.shape[0] // CLUSTER
     scale = 2.0 / width * TO_BASE2
 
     def key_peer(r):
         return lax.rem(k + r, keys)
+
+    pairs = ((src_hbm, gs.at[k]), (sw_hbm, sw_ref), (tgt_hbm, tgt_ref), (td_hbm, td_ref),
+             (pb_hbm, pb_ref), (tw_hbm, tw_ref))
+    loads = [pltpu.make_async_copy(a, b, load_sem.at[n]) for n, (a, b) in enumerate(pairs)]
+    for load in loads:
+        load.start()
 
     barrier = pltpu.get_barrier_semaphore()
 
@@ -77,15 +83,17 @@
     lax.fori_loop(1, keys, greet, 0)
     for r in range(1, groups):
         pl.semaphore_signal(barrier, inc=1, device_id=(lax.rem(g + r, groups), k), device_id_type=MESH)
-    gs[k] = src_ref[...]
+    loads[0].wait()
+    loads[1].wait()
     wg[k] = jnp.log(jnp.concatenate([sw_ref[0:1, :], sw_ref[1:2, :]], axis=1)) * LOG2E
     pl.semaphore_wait(barrier, keys + groups - 2)
 
-    def shard(slot, lane):
+    def shard(slot, lane, part):
         target = (2 * (pos - 1) + core, 2 * (pos + 1) + core, 2 * pos + 1 - core)[lane]
-        return pltpu.make_async_remote_copy(
-            src_ref=gs.at[slot], dst_ref=gs.at[slot], send_sem=s_send.at[lane, slot],
-            recv_sem=s_recv.at[slot], device_id=(g, target), device_id_type=MESH)
+        piece = gs.at[slot, pl.ds(pl.multiple_of(part * HALF, HALF), HALF)]
+        return pltpu.make_async_remote_copy(
+            src_ref=piece, dst_ref=piece, send_sem=s_send.at[lane, slot, part],
+            recv_sem=s_recv.at[slot, part], device_id=(g, target), device_id_type=MESH)
 
     def weights(r):
         return pltpu.make_async_remote_copy(
@@ -98,21 +106,28 @@
             src_ref=wg.at[peer], dst_ref=wg.at[peer], send_sem=w_send.at[r], recv_sem=w_recv.at[peer],
             device_id=(g, peer), device_id_type=MESH)
 
-    @pl.when(pos > 0)
-    def _():
-        shard(k, 0).start()
-
-    @pl.when(pos < n_pos - 1)
-    def _():
-        shard(k, 1).start()
-
-    shard(k, 2).start()
+    def send_own(part, carry):
+        @pl.when(pos > 0)
+        def _():
+            shard(k, 0, part).start()
+
+        @pl.when(pos < n_pos - 1)
+        def _():
+            shard(k, 1, part).start()
+
+        shard(k, 2, part).start()
+        return carry
+
+    lax.fori_loop(0, 2, send_own, 0)
 
     def send_weights(r, carry):
         weights(r).start()
         return carry
 
     lax.fori_loop(1, keys, send_weights, 0)
+
+    for load in loads[2:]:
+        load.wait()
 
     def prepare(t, carry):
         sq = square_row(tgt_ref[pl.ds(pl.multiple_of(t * CLUSTER, CLUSTER), CLUSTER), :])
@@ -142,50 +157,53 @@
         listed = listed_rows(n_tgt, tgt_ids, src_ids, slot)
         plse[k, pl.ds(slot, 1), :] = merge(mt[0:n_tgt, :], lt[0:n_tgt, :], listed)
 
-    def distance(d, carry):
+    def stage(n, carry):
+        d, part = n // 2, n % 2
         before, after = pos - d, pos + d
 
         @pl.when((d > 0) & (before >= 0))
         def _():
             slot = 2 * before + core
-            shard(slot, 1).wait_recv()
+            shard(slot, 1, part).wait_recv()
 
             @pl.when(pos < n_pos - 1)
             def _():
-                shard(slot, 1).start()
-
-            shard(slot, 2).start()
+                shard(slot, 1, part).start()
+
+            shard(slot, 2, part).start()
 
         @pl.when((d > 0) & (after < n_pos))
         def _():
             slot = 2 * after + core
-            shard(slot, 0).wait_recv()
+            shard(slot, 0, part).wait_recv()
 
             @pl.when(pos > 0)
             def _():
-                shard(slot, 0).start()
-
-            shard(slot, 2).start()
-
-        def job(w, carry):
-            forward, other = w % 2, w // 2
-            at = pos + d * (2 * forward - 1)
-
-            @pl.when((at >= 0) & (at < n_pos) & ((d > 0) | (forward == 0)))
-            def _():
-                slot = 2 * at + core + other * (1 - 2 * core)
-
-                @pl.when(other == 1)
+                shard(slot, 0, part).start()
+
+            shard(slot, 2, part).start()
+
+        far = d - 1 + part
+
+        def job(forward, carry):
+            at = pos + far * (2 * forward - 1)
+
+            @pl.when((at >= 0) & (at < n_pos) & (far >= forward))
+            def _():
+                slot = 2 * at + core + (1 - part) * (1 - 2 * core)
+
+                @pl.when(part == 0)
                 def _():
-                    shard(slot, 2).wait_recv()
+                    shard(slot, 2, 0).wait_recv()
+                    shard(slot, 2, 1).wait_recv()
 
                 first(slot)
 
             return carry
 
-        return lax.fori_loop(0, 4, job, carry)
-
-    lax.fori_loop(0, n_pos, distance, 0)
+        return lax.fori_loop(0, 2, job, carry)
+
+    lax.fori_loop(1, 2 * n_pos + 1, stage, 0)
 
     def partial(r):
         return pltpu.make_async_remote_copy(
@@ -208,7 +226,7 @@
         return carry
 
     lax.fori_loop(1, keys, send_partial, 0)
-    own_sq = square_row(src_ref[...])
+    own_sq = square_row(gs[k])
     lax.fori_loop(1, keys, take_partial, 0)
 
     every = plse[...]
@@ -246,7 +264,7 @@
         tl[g, pl.ds(t, 1), :] = merge(mt[0:keys, :], lt[0:keys, :], listed)
         return carry
 
-    lax.fori_loop(0, n_tgt, second, 0)
+    lax.fori_loop(0, n_tgt, second, 0, unroll=2)
 
     def column(r):
         return pltpu.make_async_remote_copy(
@@ -264,16 +282,17 @@
 
     def sent_shards(p, carry):
         slot = 2 * p + core
-
-        @pl.when((pos > 0) & (p >= pos))
-        def _():
-            shard(slot, 0).wait_send()
-
-        @pl.when((pos < n_pos - 1) & (p <= pos))
-        def _():
-            shard(slot, 1).wait_send()
-
-        shard(slot, 2).wait_send()
+        for part in range(2):
+
+            @pl.when((pos > 0) & (p >= pos))
+            def _():
+                shard(slot, 0, part).wait_send()
+
+            @pl.when((pos < n_pos - 1) & (p <= pos))
+            def _():
+                shard(slot, 1, part).wait_send()
+
+            shard(slot, 2, part).wait_send()
         return carry
 
     def sent_rows(r, carry):
@@ -312,9 +331,15 @@
         functools.partial(kernel, groups, keys),
         out_shape=(jax.ShapeDtypeStruct((CLUSTER // HALF, HALF), f32),
                    jax.ShapeDtypeStruct((rows // HALF, HALF), f32)),
-        in_specs=[pl.BlockSpec(memory_space=pltpu.VMEM)] * 7,
+        in_specs=[pl.BlockSpec(memory_space=pltpu.HBM)] * 6 + [pl.BlockSpec(memory_space=pltpu.VMEM)],
         out_specs=[pl.BlockSpec(memory_space=pltpu.VMEM)] * 2,
         scratch_shapes=[
+            pltpu.VMEM((rows, width), jnp.bfloat16),
+            pltpu.VMEM((CLUSTER // HALF, HALF), f32),
+            pltpu.VMEM((rows // HALF, HALF), f32),
+            pltpu.VMEM((rows // HALF, HALF), f32),
+            pltpu.VMEM((2, slots), jnp.int32),
+            dma((6,)),
             pltpu.VMEM((keys, CLUSTER, width), jnp.bfloat16),
             pltpu.VMEM((keys, keys, CLUSTER), f32),
             pltpu.VMEM((keys, 1, CLUSTER), f32),
@@ -325,13 +350,13 @@
             pltpu.VMEM((n_tgt, CLUSTER), f32),
             pltpu.VMEM((most, CLUSTER), f32),
             pltpu.VMEM((most, CLUSTER), f32),
-            dma((3, keys)), dma((keys,)),
+            dma((3, keys, 2)), dma((keys, 2)),
             dma((keys,)), dma((keys,)),
             dma((keys,)), dma((keys,)),
             dma((groups,)), dma((groups,)),
         ],
         compiler_params=pltpu.CompilerParams(
-            collective_id=0, has_side_effects=True, vmem_limit_bytes=44 * 1024 * 1024),
+            collective_id=0, has_side_effects=True, vmem_limit_bytes=63 * 1024 * 1024),
         cost_estimate=pl.CostEstimate(
             flops=blocks * 2 * CLUSTER * CLUSTER * width, bytes_accessed=2 * rows * width,
             transcendentals=blocks * CLUSTER * CLUSTER),

time: 42.3 us -> 38.4 us (0.908)
  local copies, waits for them, and re-layouts: 5.34 us -> 1.84 us
    unnamed x14 -> x4, local copies, waits for them, and re-layouts: 5.34 us -> 1.84 us
where the time goes in v1:
time: 38.4 us; the launch traced here: 38.2 us
  Pallas kernels  35.1 us (91%)
  local copies, waits for them, and re-layouts  1.84 us (5%)
  between operations  1.3 us (3%)
    pallas_call x1, Pallas kernels, local(): pl.pallas_call(functools.partial(kernel, groups, keys), out_shape=(jax.Sh...  35.1 us
    unnamed x4, local copies, waits for them, and re-layouts  1.84 us

profile of v1, /device:TPU:0, one launch (start us, length us, event | category | flops | bytes accessed | tf_op | source)
XLA Modules:
  0.0 38.2 jit_solution(9071686795085599315)
XLA Ops:
  1.3 35.1 %shard_map.86 = (f32[2,128]{1,0:T(2,128)}, f32[16,128]{1,0:T(8,128)}) custom-call(bf16[256,256]{1,0:T(8,128)(2,1)} %src_hbm.1, bf16[2048,256]{1,0:T(8,128)(2,1)} %tgt_hbm.1, f32[2,128]{1,0:T(2,128)} %bitcast.10, f32[16,128]{1,0:T(8,128)} %bitcast.8, f32[16,128]{1,0:T(8,128)} %bitcast.9, s32[2,64]{1,0:T(2,128)} %bitcast.11, s32[1,1]{1,0:T(1,128)S(6)} %copy.11.pc_ref), custom_call_target="tpu_custom_call" | custom-call | flops 4294967296 | bytes 1048576 | tf_op jit(solution)/shard_map/pallas_call | solution.py:330
  36.4 0.0 copy-start
  36.4 1.2 %copy.12 = f32[256]{0:T(256)} copy(f32[256]{0:T(256)} %bitcast.7) | data formatting | bytes 2048
  37.6 0.0 copy-done
  37.6 0.6 %copy.13 = f32[2048]{0:T(1024)} copy(f32[2048]{0:T(1024)S(1)} %bitcast.6) | data formatting | bytes 16384
Async XLA Ops:
  36.4 1.2 %copy-start = (f32[16,128]{1,0:T(8,128)S(1)}, f32[16,128]{1,0:T(8,128)}, u32[]{:S(2)}) copy-start(f32[16,128]{1,0:T(8,128)} %get-tuple-element.5) | copy-start | bytes 24580

commit v2 on v1

--- a/solution.py
+++ b/solution.py
@@ -12,9 +12,9 @@
 HALF = 128
 ENTROPY = 0.05
 NEG_FLOOR = -1e30
-LOG2E = 1.0 / math.log(2.0)
-TO_BASE2 = LOG2E / ENTROPY
-FROM_BASE2 = ENTROPY / LOG2E
+LANES = 8
+CHUNK = 128
+PARTS = CLUSTER // CHUNK * LANES
 MESH = pl.DeviceIdType.MESH
 NT = (((1,), (1,)), ((), ()))
 
@@ -36,23 +36,24 @@
     return jnp.broadcast_to(row, (HALF, HALF)).T
 
 
-def block_sums(left, right, scale, offset_ref, start):
-    inner = nt_dot(left, right) * scale
-    offset = offset_ref[pl.ds(start, CLUSTER), :]
-    tops, totals = [], []
-    for half in range(CLUSTER // HALF):
-        score = inner[:, half * HALF : (half + 1) * HALF] + offset
-        top = jnp.max(score, axis=0, keepdims=True)
-        totals.append(jnp.sum(jnp.exp2(score - top), axis=0, keepdims=True))
-        tops.append(top)
-    return jnp.concatenate(tops, axis=1), jnp.concatenate(totals, axis=1)
+def block_sums(left, right, scale, offset_ref, start, tops, totals, row):
+    inner = nt_dot(left, right)
+    for c in range(CLUSTER // CHUNK):
+        rows = slice(c * CHUNK, (c + 1) * CHUNK)
+        offset = offset_ref[pl.ds(start + c * CHUNK, CHUNK), :]
+        for half in range(CLUSTER // HALF):
+            lanes = slice(half * HALF, (half + 1) * HALF)
+            score = (inner[rows, lanes] + offset).reshape(CHUNK // LANES, LANES, HALF)
+            top = jnp.max(score, axis=0)
+            tops[pl.ds(row + c * LANES, LANES), lanes] = top
+            totals[pl.ds(row + c * LANES, LANES), lanes] = jnp.sum(jnp.exp((score - top) * scale), axis=0)
 
 
 def merge(tops, totals, listed):
     tops = jnp.where(listed, tops, NEG_FLOOR)
     best = jnp.max(tops, axis=0, keepdims=True)
-    total = jnp.sum(jnp.where(listed, totals * jnp.exp2(tops - best), 0.0), axis=0, keepdims=True)
-    return best + jnp.log(total) * LOG2E
+    total = jnp.sum(jnp.where(listed, totals * jnp.exp(tops - best), 0.0), axis=0, keepdims=True)
+    return best + jnp.log(total)
 
 
 def kernel(groups, keys, src_hbm, tgt_hbm, sw_hbm, tw_hbm, td_hbm, pb_hbm, pc_ref, so_ref, to_ref,
@@ -63,7 +64,7 @@
     n_pos = keys // 2
     width = tgt_ref.shape[1]
     n_tgt = tgt_ref.shape[0] // CLUSTER
-    scale = 2.0 / width * TO_BASE2
+    scale = 2.0 / width / ENTROPY
 
     def key_peer(r):
         return lax.rem(k + r, keys)
@@ -85,7 +86,7 @@
         pl.semaphore_signal(barrier, inc=1, device_id=(lax.rem(g + r, groups), k), device_id_type=MESH)
     loads[0].wait()
     loads[1].wait()
-    wg[k] = jnp.log(jnp.concatenate([sw_ref[0:1, :], sw_ref[1:2, :]], axis=1)) * LOG2E
+    wg[k] = jnp.log(jnp.concatenate([sw_ref[0:1, :], sw_ref[1:2, :]], axis=1))
     pl.semaphore_wait(barrier, keys + groups - 2)
 
     def shard(slot, lane, part):
@@ -133,7 +134,7 @@
         sq = square_row(tgt_ref[pl.ds(pl.multiple_of(t * CLUSTER, CLUSTER), CLUSTER), :])
         sqt[pl.ds(t, 1), :] = sq
         for half in range(2):
-            row = (td_ref[pl.ds(2 * t + half, 1), :] - sq[:, half * HALF : (half + 1) * HALF]) * TO_BASE2
+            row = (td_ref[pl.ds(2 * t + half, 1), :] - sq[:, half * HALF : (half + 1) * HALF]) * (0.5 * width)
             acol[pl.ds(pl.multiple_of(t * CLUSTER + half * HALF, HALF), HALF), :] = spread(row)
         return carry
 
@@ -145,17 +146,16 @@
     tgt_ids = pb_ref[1:2, :]
 
     def listed_rows(rows, row_ids, other_ids, other):
-        hit = (lax.broadcasted_iota(jnp.int32, (rows, slots), 0) == row_ids) & (other_ids == other)
+        cluster = lax.broadcasted_iota(jnp.int32, (rows * PARTS, slots), 0) // PARTS
+        hit = (cluster == row_ids) & (other_ids == other)
         return jnp.sum(jnp.where(hit, 1.0, 0.0), axis=1, keepdims=True) > 0.0
 
     def first(slot):
         src = gs[slot]
         for t in range(n_tgt):
-            top, total = block_sums(tgt_ref[t * CLUSTER : (t + 1) * CLUSTER, :], src, scale, acol, t * CLUSTER)
-            mt[t : t + 1, :] = top
-            lt[t : t + 1, :] = total
+            block_sums(tgt_ref[t * CLUSTER : (t + 1) * CLUSTER, :], src, scale, acol, t * CLUSTER, mt, lt, t * PARTS)
         listed = listed_rows(n_tgt, tgt_ids, src_ids, slot)
-        plse[k, pl.ds(slot, 1), :] = merge(mt[0:n_tgt, :], lt[0:n_tgt, :], listed)
+        plse[k, pl.ds(slot, 1), :] = merge(mt[0 : n_tgt * PARTS, :] * scale, lt[0 : n_tgt * PARTS, :], listed)
 
     def stage(n, carry):
         d, part = n // 2, n % 2
@@ -231,14 +231,14 @@
 
     every = plse[...]
     best = jnp.max(every, axis=0)
-    total = jnp.sum(jnp.exp2(every - best[None]), axis=0)
-    brow[...] = wg[...].reshape(keys, CLUSTER) - (best + jnp.log(total) * LOG2E)
-    own = brow[pl.ds(k, 1), :] * FROM_BASE2 + own_sq
+    total = jnp.sum(jnp.exp(every - best[None]), axis=0)
+    brow[...] = wg[...].reshape(keys, CLUSTER) - (best + jnp.log(total))
+    own = brow[pl.ds(k, 1), :] * ENTROPY + own_sq
     so_ref[0:1, :] = own[:, :HALF]
     so_ref[1:2, :] = own[:, HALF:]
 
     def columns(s, carry):
-        row = brow[pl.ds(s, 1), :]
+        row = brow[pl.ds(s, 1), :] * (0.5 * width * ENTROPY)
         for half in range(2):
             bcol[pl.ds(pl.multiple_of(s * CLUSTER + half * HALF, HALF), HALF), :] = spread(
                 row[:, half * HALF : (half + 1) * HALF])
@@ -254,14 +254,13 @@
         def some(c, carry):
             for j in range(step):
                 s = c * step + j
-                top, total = block_sums(gs[s], tgt, scale, bcol, pl.multiple_of(s * CLUSTER, CLUSTER))
-                mt[pl.ds(s, 1), :] = top
-                lt[pl.ds(s, 1), :] = total
+                block_sums(gs[s], tgt, scale, bcol, pl.multiple_of(s * CLUSTER, CLUSTER), mt, lt,
+                           pl.multiple_of(s * PARTS, PARTS))
             return carry
 
         lax.fori_loop(0, keys // step, some, 0)
         listed = listed_rows(keys, src_ids, tgt_ids, t)
-        tl[g, pl.ds(t, 1), :] = merge(mt[0:keys, :], lt[0:keys, :], listed)
+        tl[g, pl.ds(t, 1), :] = merge(mt[0 : keys * PARTS, :] * scale, lt[0 : keys * PARTS, :], listed)
         return carry
 
     lax.fori_loop(0, n_tgt, second, 0, unroll=2)
@@ -307,9 +306,9 @@
 
     every = tl[...]
     best = jnp.max(every, axis=0)
-    total = jnp.sum(jnp.exp2(every - best[None]), axis=0)
-    lse = best + jnp.log(total) * LOG2E
-    new = sqt[...] - lse * FROM_BASE2
+    total = jnp.sum(jnp.exp(every - best[None]), axis=0)
+    lse = best + jnp.log(total)
+    new = sqt[...] - lse * ENTROPY
     for t in range(n_tgt):
         for half in range(2):
             at = 2 * t + half
@@ -348,8 +347,8 @@
             pltpu.VMEM((keys * CLUSTER, HALF), f32),
             pltpu.VMEM((keys, CLUSTER), f32),
             pltpu.VMEM((n_tgt, CLUSTER), f32),
-            pltpu.VMEM((most, CLUSTER), f32),
-            pltpu.VMEM((most, CLUSTER), f32),
+            pltpu.VMEM((most * PARTS, CLUSTER), f32),
+            pltpu.VMEM((most * PARTS, CLUSTER), f32),
             dma((3, keys, 2)), dma((keys, 2)),
             dma((keys,)), dma((keys,)),
             dma((keys,)), dma((keys,)),

time: 38.4 us -> 38.9 us (1.013)
  Pallas kernels: 35.1 us -> 35.6 us
    pallas_call x1, Pallas kernels: 35.1 us -> 35.6 us  [local(): pl.pallas_call(functools.partial(kernel, groups, keys), out_shape=(jax.Sh...]
where the time goes in v2:
time: 38.9 us; the launch traced here: 38.7 us
  Pallas kernels  35.6 us (92%)
  local copies, waits for them, and re-layouts  1.84 us (5%)
  between operations  1.3 us (3%)
    pallas_call x1, Pallas kernels, local(): pl.pallas_call(functools.partial(kernel, groups, keys), out_shape=(jax.Sh...  35.6 us
    unnamed x4, local copies, waits for them, and re-layouts  1.84 us

profile of v2, /device:TPU:0, one launch (start us, length us, event | category | flops | bytes accessed | tf_op | source)
XLA Modules:
  0.0 38.7 jit_solution(10265095159865646540)
XLA Ops:
  1.3 35.6 %shard_map.86 = (f32[2,128]{1,0:T(2,128)}, f32[16,128]{1,0:T(8,128)}) custom-call(bf16[256,256]{1,0:T(8,128)(2,1)} %src_hbm.1, bf16[2048,256]{1,0:T(8,128)(2,1)} %tgt_hbm.1, f32[2,128]{1,0:T(2,128)} %bitcast.10, f32[16,128]{1,0:T(8,128)} %bitcast.8, f32[16,128]{1,0:T(8,128)} %bitcast.9, s32[2,64]{1,0:T(2,128)} %bitcast.11, s32[1,1]{1,0:T(1,128)S(6)} %copy.11.pc_ref), custom_call_target="tpu_custom_call" | custom-call | flops 4294967296 | bytes 1048576 | tf_op jit(solution)/shard_map/pallas_call | solution.py:329
  36.8 0.0 copy-start
  36.9 1.2 %copy.12 = f32[256]{0:T(256)} copy(f32[256]{0:T(256)} %bitcast.7) | data formatting | bytes 2048
  38.1 0.0 copy-done
  38.1 0.6 %copy.13 = f32[2048]{0:T(1024)} copy(f32[2048]{0:T(1024)S(1)} %bitcast.6) | data formatting | bytes 16384
Async XLA Ops:
  36.8 1.2 %copy-start = (f32[16,128]{1,0:T(8,128)S(1)}, f32[16,128]{1,0:T(8,128)}, u32[]{:S(2)}) copy-start(f32[16,128]{1,0:T(8,128)} %get-tuple-element.5) | copy-start | bytes 24580

commit v3 on v2

--- a/solution.py
+++ b/solution.py
@@ -38,7 +38,7 @@
 
 def block_sums(left, right, scale, offset_ref, start, tops, totals, row):
     inner = nt_dot(left, right)
-    for c in range(CLUSTER // CHUNK):
+    for c in range(left.shape[0] // CHUNK):
         rows = slice(c * CHUNK, (c + 1) * CHUNK)
         offset = offset_ref[pl.ds(start + c * CHUNK, CHUNK), :]
         for half in range(CLUSTER // HALF):
@@ -152,8 +152,7 @@
 
     def first(slot):
         src = gs[slot]
-        for t in range(n_tgt):
-            block_sums(tgt_ref[t * CLUSTER : (t + 1) * CLUSTER, :], src, scale, acol, t * CLUSTER, mt, lt, t * PARTS)
+        block_sums(tgt_ref[...], src, scale, acol, 0, mt, lt, 0)
         listed = listed_rows(n_tgt, tgt_ids, src_ids, slot)
         plse[k, pl.ds(slot, 1), :] = merge(mt[0 : n_tgt * PARTS, :] * scale, lt[0 : n_tgt * PARTS, :], listed)
 
@@ -252,10 +251,9 @@
         tgt = tgt_ref[pl.ds(pl.multiple_of(t * CLUSTER, CLUSTER), CLUSTER), :]
 
         def some(c, carry):
-            for j in range(step):
-                s = c * step + j
-                block_sums(gs[s], tgt, scale, bcol, pl.multiple_of(s * CLUSTER, CLUSTER), mt, lt,
-                           pl.multiple_of(s * PARTS, PARTS))
+            some_src = gs[pl.ds(c * step, step)].reshape(step * CLUSTER, width)
+            block_sums(some_src, tgt, scale, bcol, pl.multiple_of(c * step * CLUSTER, CLUSTER), mt, lt,
+                       pl.multiple_of(c * step * PARTS, PARTS))
             return carry
 
         lax.fori_loop(0, keys // step, some, 0)

time: 38.9 us -> 38.6 us (level)
  no operation moved by 1% of the time
where the time goes in v3:
time: 38.6 us; the launch traced here: 38.4 us
  Pallas kernels  35.3 us (91%)
  local copies, waits for them, and re-layouts  1.84 us (5%)
  between operations  1.3 us (3%)
    pallas_call x1, Pallas kernels, local(): pl.pallas_call(functools.partial(kernel, groups, keys), out_shape=(jax.Sh...  35.3 us
    unnamed x4, local copies, waits for them, and re-layouts  1.84 us

profile of v3, /device:TPU:0, one launch (start us, length us, event | category | flops | bytes accessed | tf_op | source)
XLA Modules:
  0.0 38.4 jit_solution(12754308436319773852)
XLA Ops:
  1.3 35.3 %shard_map.86 = (f32[2,128]{1,0:T(2,128)}, f32[16,128]{1,0:T(8,128)}) custom-call(bf16[256,256]{1,0:T(8,128)(2,1)} %src_hbm.1, bf16[2048,256]{1,0:T(8,128)(2,1)} %tgt_hbm.1, f32[2,128]{1,0:T(2,128)} %bitcast.10, f32[16,128]{1,0:T(8,128)} %bitcast.8, f32[16,128]{1,0:T(8,128)} %bitcast.9, s32[2,64]{1,0:T(2,128)} %bitcast.11, s32[1,1]{1,0:T(1,128)S(6)} %copy.11.pc_ref), custom_call_target="tpu_custom_call" | custom-call | flops 4294967296 | bytes 1048576 | tf_op jit(solution)/shard_map/pallas_call | solution.py:327
  36.6 0.0 copy-start
  36.6 1.2 %copy.12 = f32[256]{0:T(256)} copy(f32[256]{0:T(256)} %bitcast.7) | data formatting | bytes 2048
  37.8 0.0 copy-done
  37.8 0.6 %copy.13 = f32[2048]{0:T(1024)} copy(f32[2048]{0:T(1024)S(1)} %bitcast.6) | data formatting | bytes 16384
Async XLA Ops:
  36.6 1.2 %copy-start = (f32[16,128]{1,0:T(8,128)S(1)}, f32[16,128]{1,0:T(8,128)}, u32[]{:S(2)}) copy-start(f32[16,128]{1,0:T(8,128)} %get-tuple-element.5) | copy-start | bytes 24580

commit v4 on v3

--- a/solution.py
+++ b/solution.py
@@ -101,12 +101,6 @@
             src_ref=wg.at[k], dst_ref=wg.at[k], send_sem=w_send.at[r], recv_sem=w_recv.at[k],
             device_id=(g, key_peer(r)), device_id_type=MESH)
 
-    def weights_from(r):
-        peer = key_peer(r)
-        return pltpu.make_async_remote_copy(
-            src_ref=wg.at[peer], dst_ref=wg.at[peer], send_sem=w_send.at[r], recv_sem=w_recv.at[peer],
-            device_id=(g, peer), device_id_type=MESH)
-
     def send_own(part, carry):
         @pl.when(pos > 0)
         def _():
@@ -154,7 +148,18 @@
         src = gs[slot]
         block_sums(tgt_ref[...], src, scale, acol, 0, mt, lt, 0)
         listed = listed_rows(n_tgt, tgt_ids, src_ids, slot)
-        plse[k, pl.ds(slot, 1), :] = merge(mt[0 : n_tgt * PARTS, :] * scale, lt[0 : n_tgt * PARTS, :], listed)
+        plse[k, slot] = merge(mt[0 : n_tgt * PARTS, :] * scale, lt[0 : n_tgt * PARTS, :], listed)
+
+    spans = ((2, keys - 4), (0, 2), (keys - 2, 2))
+
+    def partial(span, sender, r):
+        low, count = spans[span]
+        piece = plse.at[sender, pl.ds(low, count)]
+        return pltpu.make_async_remote_copy(
+            src_ref=piece, dst_ref=piece, send_sem=p_send.at[span, r], recv_sem=p_recv.at[span, sender],
+            device_id=(g, key_peer(r)), device_id_type=MESH)
+
+    inner_far = jnp.maximum(jnp.abs(pos - 1), jnp.abs(n_pos - 2 - pos))
 
     def stage(n, carry):
         d, part = n // 2, n % 2
@@ -200,68 +205,94 @@
 
             return carry
 
-        return lax.fori_loop(0, 2, job, carry)
+        lax.fori_loop(0, 2, job, 0)
+
+        @pl.when(n == 2 * (inner_far + 1))
+        def _():
+            def send_inner(r, carry):
+                partial(0, k, r).start()
+                return carry
+
+            lax.fori_loop(1, keys, send_inner, 0)
+
+        return carry
 
     lax.fori_loop(1, 2 * n_pos + 1, stage, 0)
 
-    def partial(r):
-        return pltpu.make_async_remote_copy(
-            src_ref=plse.at[k], dst_ref=plse.at[k], send_sem=p_send.at[r], recv_sem=p_recv.at[k],
-            device_id=(g, key_peer(r)), device_id_type=MESH)
-
-    def partial_from(r):
-        peer = key_peer(r)
-        return pltpu.make_async_remote_copy(
-            src_ref=plse.at[peer], dst_ref=plse.at[peer], send_sem=p_send.at[r], recv_sem=p_recv.at[peer],
-            device_id=(g, peer), device_id_type=MESH)
-
-    def send_partial(r, carry):
-        partial(r).start()
-        return carry
-
-    def take_partial(r, carry):
-        weights_from(r).wait_recv()
-        partial_from(r).wait_recv()
-        return carry
-
-    lax.fori_loop(1, keys, send_partial, 0)
+    def send_outer(r, carry):
+        partial(1, k, r).start()
+        partial(2, k, r).start()
+        return carry
+
+    lax.fori_loop(1, keys, send_outer, 0)
+
+    def potentials(span):
+        low, count = spans[span]
+
+        def potential(s, carry):
+            every = plse[:, s]
+            best = jnp.max(every, axis=0)
+            row = wg[s] - (best + jnp.log(jnp.sum(jnp.exp(every - best[None]), axis=0)))
+            brow[s] = row
+            row = row * (0.5 * width * ENTROPY)
+            for half in range(2):
+                bcol[pl.ds(pl.multiple_of(s * CLUSTER + half * HALF, HALF), HALF), :] = spread(
+                    row[:, half * HALF : (half + 1) * HALF])
+            return carry
+
+        lax.fori_loop(low, low + count, potential, 0, unroll=2)
+
+    def sweep(span):
+        low, count = spans[span]
+        step = math.gcd(count, 4)
+
+        def second(t, carry):
+            tgt = tgt_ref[pl.ds(pl.multiple_of(t * CLUSTER, CLUSTER), CLUSTER), :]
+
+            def some(c, carry):
+                s = low + c * step
+                some_src = gs[pl.ds(s, step)].reshape(step * CLUSTER, width)
+                block_sums(some_src, tgt, scale, bcol, pl.multiple_of(s * CLUSTER, CLUSTER), mt, lt,
+                           pl.multiple_of((t * keys + s) * PARTS, PARTS))
+                return carry
+
+            return lax.fori_loop(0, count // step, some, carry)
+
+        lax.fori_loop(0, n_tgt, second, 0, unroll=2)
+
     own_sq = square_row(gs[k])
-    lax.fori_loop(1, keys, take_partial, 0)
-
-    every = plse[...]
-    best = jnp.max(every, axis=0)
-    total = jnp.sum(jnp.exp(every - best[None]), axis=0)
-    brow[...] = wg[...].reshape(keys, CLUSTER) - (best + jnp.log(total))
-    own = brow[pl.ds(k, 1), :] * ENTROPY + own_sq
+
+    def take_inner(r, carry):
+        pltpu.make_async_remote_copy(
+            src_ref=wg.at[key_peer(r)], dst_ref=wg.at[key_peer(r)], send_sem=w_send.at[r],
+            recv_sem=w_recv.at[key_peer(r)], device_id=(g, key_peer(r)), device_id_type=MESH).wait_recv()
+        partial(0, key_peer(r), r).wait_recv()
+        return carry
+
+    lax.fori_loop(1, keys, take_inner, 0)
+    potentials(0)
+    sweep(0)
+
+    def take_outer(r, carry):
+        partial(1, key_peer(r), r).wait_recv()
+        partial(2, key_peer(r), r).wait_recv()
+        return carry
+
+    lax.fori_loop(1, keys, take_outer, 0)
+    for span in (1, 2):
+        potentials(span)
+        sweep(span)
+    own = brow[k] * ENTROPY + own_sq
     so_ref[0:1, :] = own[:, :HALF]
     so_ref[1:2, :] = own[:, HALF:]
 
-    def columns(s, carry):
-        row = brow[pl.ds(s, 1), :] * (0.5 * width * ENTROPY)
-        for half in range(2):
-            bcol[pl.ds(pl.multiple_of(s * CLUSTER + half * HALF, HALF), HALF), :] = spread(
-                row[:, half * HALF : (half + 1) * HALF])
-        return carry
-
-    lax.fori_loop(0, keys, columns, 0)
-
-    step = math.gcd(keys, 8)
-
-    def second(t, carry):
-        tgt = tgt_ref[pl.ds(pl.multiple_of(t * CLUSTER, CLUSTER), CLUSTER), :]
-
-        def some(c, carry):
-            some_src = gs[pl.ds(c * step, step)].reshape(step * CLUSTER, width)
-            block_sums(some_src, tgt, scale, bcol, pl.multiple_of(c * step * CLUSTER, CLUSTER), mt, lt,
-                       pl.multiple_of(c * step * PARTS, PARTS))
-            return carry
-
-        lax.fori_loop(0, keys // step, some, 0)
+    def columns(t, carry):
         listed = listed_rows(keys, src_ids, tgt_ids, t)
-        tl[g, pl.ds(t, 1), :] = merge(mt[0 : keys * PARTS, :] * scale, lt[0 : keys * PARTS, :], listed)
-        return carry
-
-    lax.fori_loop(0, n_tgt, second, 0, unroll=2)
+        rows = pl.ds(pl.multiple_of(t * keys * PARTS, PARTS), keys * PARTS)
+        tl[g, pl.ds(t, 1), :] = merge(mt[rows, :] * scale, lt[rows, :], listed)
+        return carry
+
+    lax.fori_loop(0, n_tgt, columns, 0, unroll=2)
 
     def column(r):
         return pltpu.make_async_remote_copy(
@@ -294,7 +325,8 @@
 
     def sent_rows(r, carry):
         weights(r).wait_send()
-        partial(r).wait_send()
+        for span in range(3):
+            partial(span, k, r).wait_send()
         return carry
 
     lax.fori_loop(0, n_pos, sent_shards, 0)
@@ -322,7 +354,6 @@
     slots = pair_blocks.shape[3]
     f32 = jnp.float32
     dma = pltpu.SemaphoreType.DMA
-    most = max(keys, n_tgt)
     blocks = 2 * keys * n_tgt
     src_dual, tgt_new = pl.pallas_call(
         functools.partial(kernel, groups, keys),
@@ -338,17 +369,17 @@
             pltpu.VMEM((2, slots), jnp.int32),
             dma((6,)),
             pltpu.VMEM((keys, CLUSTER, width), jnp.bfloat16),
-            pltpu.VMEM((keys, keys, CLUSTER), f32),
+            pltpu.VMEM((keys, keys, 1, CLUSTER), f32),
             pltpu.VMEM((keys, 1, CLUSTER), f32),
             pltpu.VMEM((groups, n_tgt, CLUSTER), f32),
             pltpu.VMEM((rows, HALF), f32),
             pltpu.VMEM((keys * CLUSTER, HALF), f32),
-            pltpu.VMEM((keys, CLUSTER), f32),
+            pltpu.VMEM((keys, 1, CLUSTER), f32),
             pltpu.VMEM((n_tgt, CLUSTER), f32),
-            pltpu.VMEM((most * PARTS, CLUSTER), f32),
-            pltpu.VMEM((most * PARTS, CLUSTER), f32),
+            pltpu.VMEM((n_tgt * keys * PARTS, CLUSTER), f32),
+            pltpu.VMEM((n_tgt * keys * PARTS, CLUSTER), f32),
             dma((3, keys, 2)), dma((keys, 2)),
-            dma((keys,)), dma((keys,)),
+            dma((3, keys)), dma((3, keys)),
             dma((keys,)), dma((keys,)),
             dma((groups,)), dma((groups,)),
         ],

time: 38.6 us -> 38.2 us (0.990)
  Pallas kernels: 35.3 us -> 34.9 us
    pallas_call x1, Pallas kernels: 35.3 us -> 34.9 us  [local(): pl.pallas_call(functools.partial(kernel, groups, keys), out_shape=(jax.Sh...]
where the time goes in v4:
time: 38.2 us; the launch traced here: 38 us
  Pallas kernels  34.9 us (91%)
  local copies, waits for them, and re-layouts  1.84 us (5%)
  between operations  1.3 us (3%)
    pallas_call x1, Pallas kernels, local(): pl.pallas_call(functools.partial(kernel, groups, keys), out_shape=(jax.Sh...  34.9 us
    unnamed x4, local copies, waits for them, and re-layouts  1.84 us

profile of v4, /device:TPU:0, one launch (start us, length us, event | category | flops | bytes accessed | tf_op | source)
XLA Modules:
  0.0 38.0 jit_solution(15320508487883455300)
XLA Ops:
  1.3 34.9 %shard_map.86 = (f32[2,128]{1,0:T(2,128)}, f32[16,128]{1,0:T(8,128)}) custom-call(bf16[256,256]{1,0:T(8,128)(2,1)} %src_hbm.1, bf16[2048,256]{1,0:T(8,128)(2,1)} %tgt_hbm.1, f32[2,128]{1,0:T(2,128)} %bitcast.10, f32[16,128]{1,0:T(8,128)} %bitcast.8, f32[16,128]{1,0:T(8,128)} %bitcast.9, s32[2,64]{1,0:T(2,128)} %bitcast.11, s32[1,1]{1,0:T(1,128)S(6)} %copy.11.pc_ref), custom_call_target="tpu_custom_call" | custom-call | flops 4294967296 | bytes 1048576 | tf_op jit(solution)/shard_map/pallas_call | solution.py:358
  36.2 0.0 copy-start
  36.2 1.2 %copy.12 = f32[256]{0:T(256)} copy(f32[256]{0:T(256)} %bitcast.7) | data formatting | bytes 2048
  37.4 0.0 copy-done
  37.4 0.6 %copy.13 = f32[2048]{0:T(1024)} copy(f32[2048]{0:T(1024)S(1)} %bitcast.6) | data formatting | bytes 16384
Async XLA Ops:
  36.2 1.2 %copy-start = (f32[16,128]{1,0:T(8,128)S(1)}, f32[16,128]{1,0:T(8,128)}, u32[]{:S(2)}) copy-start(f32[16,128]{1,0:T(8,128)} %get-tuple-element.5) | copy-start | bytes 24580
